TPU v7x, 128 devices: a whole 4x4x4 slice. The times are simulated.
128 devices in a mesh: dp: 8 (over x, y_lo), tensor: 16 (over z, y_hi, core).
Axes of the slice: x: 4, y: 4 (y_hi: 2, y_lo: 2; y = y_hi * 2 + y_lo), z: 4, core: 2. Of those that a mesh axis runs over, the one named last changes fastest.
Arguments:
- inputs: bfloat16 [8192, 9216], P(('dp', 'tensor')), may hold values from -8.5 to 8.5
- queries: bfloat16 [8192, 9216], P('dp', 'tensor'), may hold values from -24 to 24
- d_attn: bfloat16 [8192, 9216], P('dp', 'tensor'), may hold values from -6 to 6
- w_key: bfloat16 [9216, 1536], P(None, 'tensor'), may hold values from -0.0625 to 0.0625
- w_value: bfloat16 [9216, 1536], P(None, 'tensor'), may hold values from -0.0625 to 0.0625
Outputs:
- d_input: bfloat16 [8192, 9216], P(('dp', 'tensor'))
- d_queries: bfloat16 [8192, 9216], P('dp', 'tensor')
- grad_key: float32 [9216, 1536], P('dp', 'tensor')
- grad_value: float32 [9216, 1536], P('dp', 'tensor')
All inputs are finite; a program needn't handle non-finite values.
Results may differ from a plain program's by a relative error of at most 0.02.
Values may be sent and summed in bfloat16 or wider, within the bound.
No kernel may reach another device: no remote copies, remote signals or barrier semaphores. Data moves between devices by JAX's collectives and lax.ppermute only.
A program may use at most 256 MiB of HBM per device.

v0:
```python
import jax
import jax.numpy as jnp
from jax import lax
from jax.sharding import PartitionSpec as P

HEAD = 192


def partner(value, axis, apart):
    mask = 2**apart
    pairs = [(source, source ^ mask) for source in range(lax.axis_size(axis))]
    return lax.ppermute(value, axis, pairs)


def body(inputs, queries, d_attn, w_key, w_value):
    seq_rows = lax.all_gather(inputs, "tensor", axis=0, tiled=True)
    length = seq_rows.shape[0]
    half_head = w_key.shape[1]
    parity = lax.axis_index("tensor") % 2

    def joined(own_part, other_part):
        return jnp.where(
            parity == 0,
            jnp.concatenate([own_part, other_part], 1),
            jnp.concatenate([other_part, own_part], 1),
        )

    def own_half(full):
        return jnp.where(parity == 0, full[:, :half_head], full[:, half_head:])

    def other_half(full):
        return jnp.where(parity == 0, full[:, half_head:], full[:, :half_head])

    key_half = jnp.dot(seq_rows, w_key, preferred_element_type=jnp.float32).astype(jnp.bfloat16)
    value_half = jnp.dot(seq_rows, w_value, preferred_element_type=jnp.float32).astype(jnp.bfloat16)
    partner_key, partner_value = partner((key_half, value_half), "tensor", 0)
    key_rows = joined(key_half, partner_key)
    value_rows = joined(value_half, partner_value)
    head_count = queries.shape[1] // HEAD
    score_scale = HEAD ** (-0.5)
    queries3 = queries.reshape(length, head_count, HEAD)
    grads3 = d_attn.reshape(length, head_count, HEAD)
    positions = jnp.arange(length)
    causal = positions[:, None] >= positions[None, :]
    scores = (
        jnp.einsum("qhd,kd->hqk", queries3, key_rows, preferred_element_type=jnp.float32)
        * score_scale
    )
    scores = jnp.where(causal, scores, -jnp.inf)
    row_max = jnp.max(scores, -1, keepdims=True)
    attention = jnp.exp(scores - row_max)
    attention = attention / jnp.sum(attention, -1, keepdims=True)
    d_probs = jnp.einsum("qhd,kd->hqk", grads3, value_rows, preferred_element_type=jnp.float32)
    row_total = jnp.sum(attention * d_probs, -1, keepdims=True)
    d_scores = (attention * (d_probs - row_total) * score_scale).astype(jnp.bfloat16)
    attention_low = attention.astype(jnp.bfloat16)
    d_query = (
        jnp.einsum("hqk,kd->qhd", d_scores, key_rows, preferred_element_type=jnp.float32)
        .astype(jnp.bfloat16)
        .reshape(length, -1)
    )
    key_part = jnp.einsum("hqk,qhd->kd", d_scores, queries3, preferred_element_type=jnp.float32)
    value_part = jnp.einsum(
        "hqk,qhd->kd", attention_low, grads3, preferred_element_type=jnp.float32
    )
    partner_kgrad, partner_vgrad = (
        partner(other_half(key_part).astype(jnp.bfloat16), "tensor", 0).astype(jnp.float32),
        partner(other_half(value_part).astype(jnp.bfloat16), "tensor", 0).astype(jnp.float32),
    )
    d_key = (own_half(key_part) + partner_kgrad).astype(jnp.bfloat16)
    d_value = (own_half(value_part) + partner_vgrad).astype(jnp.bfloat16)
    d_all = jnp.concatenate([d_key, d_value], 1)
    w_all = jnp.concatenate([w_key, w_value], 1)
    block = d_all
    d_input = lax.psum_scatter(
        lax.dot_general(
            block, w_all, (((1,), (1,)), ((), ())), preferred_element_type=jnp.float32
        ).astype(jnp.bfloat16),
        "tensor",
        scatter_dimension=0,
        tiled=True,
    )
    block = seq_rows
    grads = lax.psum_scatter(
        lax.dot_general(
            block, d_all, (((0,), (0,)), ((), ())), preferred_element_type=jnp.float32
        ).astype(jnp.bfloat16),
        "dp",
        scatter_dimension=0,
        tiled=True,
    ).astype(jnp.float32)
    return (d_input, d_query, grads[:, :half_head], grads[:, half_head:])


def solution(mesh):
    placed = (
        P(("dp", "tensor"), None),
        P("dp", "tensor"),
        P("dp", "tensor"),
        P(None, "tensor"),
        P(None, "tensor"),
    )
    return jax.shard_map(
        body,
        mesh=mesh,
        in_specs=placed,
        out_specs=(
            P(("dp", "tensor"), None),
            P("dp", "tensor"),
            P("dp", "tensor"),
            P("dp", "tensor"),
        ),
        check_vma=False,
    )
```

profile of v0, /device:TPU:22, one launch (start us, length us, event | category | flops | bytes accessed | tf_op | source)
XLA Modules:
  0.0 481.7 jit_solution(10699957086558201964)
XLA Ops:
  7.2 0.0 copy-start
  7.2 0.0 copy-start.3
  7.2 0.0 all-gather.2.cloned.1.call-start
  7.2 0.7 all-gather.2.cloned.1.call-update
  7.9 0.0 reduce-scatter.7.cloned.1.call-start
  8.0 1.3 iota_compare_fusion
  9.3 119.9 %all-gather.2.cloned.1.call-done = bf16[1024,9216]{1,0:T(8,128)(2,1)} async-done(((bf16[64,9216]{1,0:T(8,128)(2,1)}), bf16[1024,9216]{1,0:T(8,128)(2,1)}) %all-gather.2.cloned.1.call-update) | async-done | bytes 18874384 | tf_op jit(solution)/shard_map/all_gather | solution.py:16
  129.2 0.0 copy-start.5
  129.2 12.9 %convolution_convert_fusion.3 = bf16[1024,96]{0,1:T(8,128)(2,1)S(1)} fusion(bf16[1024,9216]{1,0:T(8,128)(2,1)} %all-gather.2.cloned.1.call-done, bf16[9216,96]{0,1:T(8,128)(2,1)} %param.8), kind=kOutput, calls=%fused_computation.30 | convolution fusion | flops 1812037632 | bytes 20840448 | tf_op jit(solution)/shard_map/dot_general | solution.py:34
  142.1 0.0 copy-start.6
  142.1 0.3 collective-permute-start
  142.5 0.0 copy-done.3
  142.5 0.0 copy-done.5
  142.5 6.6 %convolution_convert_fusion.2 = bf16[1024,96]{0,1:T(8,128)(2,1)} fusion(bf16[1024,9216]{1,0:T(8,128)(2,1)S(1)} %copy-done.5, bf16[9216,96]{0,1:T(8,128)(2,1)S(1)} %copy-done.3), kind=kOutput, calls=%fused_computation.29 | convolution fusion | flops 1812037632 | bytes 20840448 | tf_op jit(solution)/shard_map/dot_general | solution.py:35
  149.1 0.3 collective-permute-start.1
  149.3 0.0 collective-permute-done
  149.3 0.0 copy-done
  149.3 0.0 copy-start.8
  149.4 0.0 copy-start.4
  149.4 8.6 %fusion.58 = (f32[3,1024]{1,0:T(4,128)S(1)}, f32[3,1024,1024]{1,2,0:T(8,128)}) fusion(pred[1024,1024]{0,1:T(8,128)(4,1)} %iota_compare_fusion, bf16[1024,3,192]{0,2,1:T(8,128)(2,1)S(1)} %bitcast.79, bf16[1024,96]{0,1:T(8,128)(2,1)S(1)} %collective-permute-done, bf16[1024,96]{0,1:T(8,128)(2,1)S(1)} %convolution_convert_fusion.3, pred[]{:T(512)S(6)} %eq.4), kind=kOutput, calls=%fused_computation.62 | convolution fusion | flops 1222312960 | bytes 15216641 | tf_op jit(solution)/shard_map/sub | solution.py:51
  157.9 0.0 copy-done.6
  157.9 0.0 copy-done.8
  157.9 0.0 copy-done.4
  157.9 6.8 %fusion.20 = f32[1024,192]{0,1:T(8,128)S(1)} fusion(bf16[1024,3,192]{0,2,1:T(8,128)(2,1)S(1)} %bitcast.81, f32[3,1024,1024]{1,2,0:T(8,128)} %get-tuple-element.7, f32[3,1024]{1,0:T(4,128)S(1)} %get-tuple-element.6), kind=kOutput, calls=%fused_computation.28 | convolution fusion | flops 1214251008 | bytes 14561280 | tf_op jit(solution)/shard_map/hqk,qhd->kd/dot_general | solution.py:63
  164.8 0.3 collective-permute-start.3
  165.2 0.0 collective-permute-done.1
  165.2 7.6 %fusion.27 = f32[1024,1024,3]{1,0,2:T(8,128)} fusion(bf16[1024,3,192]{0,2,1:T(8,128)(2,1)S(1)} %bitcast.82, bf16[1024,96]{0,1:T(8,128)(2,1)} %collective-permute-done.1, bf16[1024,96]{0,1:T(8,128)(2,1)} %convolution_convert_fusion.2, pred[]{:T(512)S(6)} %eq.4), kind=kOutput, calls=%fused_computation.36 | convolution fusion | flops 1209729024 | bytes 14155777 | tf_op jit(solution)/shard_map/qhd,kd->hqk/dot_general | solution.py:53
  172.7 19.8 %fusion.19 = f32[1024,192]{0,1:T(8,128)S(1)} fusion(bf16[1024,3,192]{0,2,1:T(8,128)(2,1)S(1)} %bitcast.80, f32[1024,1024,3]{1,0,2:T(8,128)} %fusion.27, f32[3,1024,1024]{1,2,0:T(8,128)} %get-tuple-element.7, f32[3,1024]{1,0:T(4,128)S(1)} %get-tuple-element.6), kind=kOutput, calls=%fused_computation.27 | convolution fusion | flops 1229983744 | bytes 27144192 | tf_op jit(solution)/shard_map/hqk,qhd->kd/dot_general | solution.py:62
  192.6 0.3 collective-permute-start.2
  192.9 0.0 collective-permute-done.3
  192.9 0.1 add_convert_fusion
  193.0 1.1 collective-permute-done.2
  194.1 0.1 add_convert_fusion.1
  194.2 0.0 copy-start.2
  194.2 12.2 %fusion.5 = bf16[9216,192]{0,1:T(8,128)(2,1)} fusion(bf16[1024,9216]{1,0:T(8,128)(2,1)} %all-gather.2.cloned.1.call-done, bf16[1024,96]{0,1:T(8,128)(2,1)S(1)} %add_convert_fusion, bf16[1024,96]{0,1:T(8,128)(2,1)S(1)} %add_convert_fusion.1), kind=kOutput, calls=%fused_computation.11 | convolution fusion | flops 3626434560 | bytes 22806528 | tf_op jit(solution)/shard_map/dot_general | solution.py:85
  206.4 6.3 %copy.18 = bf16[9216,192]{1,0:T(8,128)(2,1)} copy(bf16[9216,192]{0,1:T(8,128)(2,1)} %fusion.5) | data formatting | bytes 7077888
  212.7 0.0 reduce-scatter.7.cloned.1.call-update
  212.7 0.3 reduce-scatter.5.cloned.1.call-start
  213.0 0.0 copy-done.2
  213.0 10.9 %convolution_convert_fusion = bf16[1024,9216]{1,0:T(8,128)(2,1)} fusion(bf16[9216,96]{0,1:T(8,128)(2,1)} %param.9, bf16[9216,96]{0,1:T(8,128)(2,1)S(1)} %copy-done.2, bf16[1024,96]{0,1:T(8,128)(2,1)S(1)} %add_convert_fusion, bf16[1024,96]{0,1:T(8,128)(2,1)S(1)} %add_convert_fusion.1), kind=kOutput, calls=%fused_computation.2 | convolution fusion | flops 3641180160 | bytes 22806528 | tf_op jit(solution)/shard_map/dot_general | solution.py:76
  223.9 0.0 copy-start.7
  223.9 0.0 copy-start.9
  223.9 0.0 reduce-scatter.5.cloned.1.call-update
  223.9 0.9 copy-done.7
  224.8 0.1 copy-done.9
  224.9 0.0 copy-start.1
  224.9 19.2 %fusion.18 = bf16[192,3,1024]{2,0,1:T(8,128)(2,1)} fusion(f32[1024,1024,3]{1,0,2:T(8,128)} %fusion.27, bf16[1024,96]{0,1:T(8,128)(2,1)S(1)} %copy-done.9, bf16[1024,96]{0,1:T(8,128)(2,1)S(1)} %copy-done.7, pred[]{:T(512)S(6)} %eq.4, f32[3,1024,1024]{1,2,0:T(8,128)} %get-tuple-element.7, f32[3,1024]{1,0:T(4,128)S(1)} %get-tuple-element.6), kind=kOutput, calls=%fused_computation.26 | convolution fusion | flops 1232343040 | bytes 26750976 | tf_op jit(solution)/shard_map/hqk,kd->qhd/dot_general | solution.py:58
  244.2 68.6 %reduce-scatter.7.cloned.1.call-done = bf16[1152,192]{1,0:T(8,128)(2,1)} async-done(((bf16[9216,192]{1,0:T(8,128)(2,1)}), bf16[1152,192]{1,0:T(8,128)(2,1)}) %reduce-scatter.7.cloned.1.call-update) | async-done | bytes 442384
  312.7 1.3 copy.19
  314.1 1.0 fusion.57
  315.0 160.1 %reduce-scatter.5.cloned.1.call-done = bf16[64,9216]{1,0:T(8,128)(2,1)} async-done(((bf16[1024,9216]{1,0:T(8,128)(2,1)}), bf16[64,9216]{1,0:T(8,128)(2,1)}) %reduce-scatter.5.cloned.1.call-update) | async-done | bytes 1179664 | tf_op jit(solution)/shard_map/reduce_scatter | solution.py:75
  475.1 0.0 copy-done.1
  (2 shorter events, 0.1 us)
Async XLA Ops:
  7.2 142.2 %copy-start = (bf16[1024,576]{0,1:T(8,128)(2,1)S(1)}, bf16[1024,576]{0,1:T(8,128)(2,1)}, u32[]{:S(2)}) copy-start(bf16[1024,576]{0,1:T(8,128)(2,1)} %param.6) | copy-start | bytes 3538948
  7.2 135.3 %copy-start.3 = (bf16[9216,96]{0,1:T(8,128)(2,1)S(1)}, bf16[9216,96]{0,1:T(8,128)(2,1)}, u32[]{:S(2)}) copy-start(bf16[9216,96]{0,1:T(8,128)(2,1)} %param.9) | copy-start | bytes 5308420
  7.2 122.0 %all-gather.2.cloned.1.call-start = ((), (), s32[]{:S(2)}) async-start(), calls=%async_computation.2 | async-start | bytes 20054016 | tf_op jit(solution)/shard_map/all_gather | solution.py:16
  7.9 304.8 %reduce-scatter.7.cloned.1.call-start = ((), (), s32[]{:S(2)}) async-start(), calls=%async_computation.4 | async-start | bytes 5308416
  129.2 13.3 %copy-start.5 = (bf16[1024,9216]{1,0:T(8,128)(2,1)S(1)}, bf16[1024,9216]{1,0:T(8,128)(2,1)}, u32[]{:S(2)}) copy-start(bf16[1024,9216]{1,0:T(8,128)(2,1)} %all-gather.2.cloned.1.call-done) | copy-start | bytes 56623108
  142.1 15.8 %copy-start.6 = (bf16[1024,96]{0,1:T(8,128)(2,1)}, bf16[1024,96]{0,1:T(8,128)(2,1)S(1)}, u32[]{:S(2)}) copy-start(bf16[1024,96]{0,1:T(8,128)(2,1)S(1)} %convolution_convert_fusion.3) | copy-start | bytes 589828
  142.1 7.2 %collective-permute-start = (bf16[1024,96]{0,1:T(8,128)(2,1)S(1)}, bf16[1024,96]{0,1:T(8,128)(2,1)S(1)}, u32[]{:S(2)}, u32[]{:S(2)}) collective-permute-start(bf16[1024,96]{0,1:T(8,128)(2,1)S(1)} %convolution_convert_fusion.3), channel_id=1, source_target_pairs={{0,1},{1,0},{2,3},{3,2},{4,5},{5,4},{6,7},{7,6},{8,9},{9,8},{10,11... | collective-permute-start | bytes 589832 | tf_op jit(solution)/shard_map/ppermute | solution.py:12
  149.1 16.1 %collective-permute-start.1 = (bf16[1024,96]{0,1:T(8,128)(2,1)}, bf16[1024,96]{0,1:T(8,128)(2,1)}, u32[]{:S(2)}, u32[]{:S(2)}) collective-permute-start(bf16[1024,96]{0,1:T(8,128)(2,1)} %convolution_convert_fusion.2), channel_id=1, source_target_pairs={{0,1},{1,0},{2,3},{3,2},{4,5},{5,4},{6,7},{7,6},{8,9},{9,8},{10,11... | collective-permute-start | bytes 589832 | tf_op jit(solution)/shard_map/ppermute | solution.py:12
  149.3 8.6 %copy-start.8 = (bf16[1024,96]{0,1:T(8,128)(2,1)}, bf16[1024,96]{0,1:T(8,128)(2,1)S(1)}, u32[]{:S(2)}) copy-start(bf16[1024,96]{0,1:T(8,128)(2,1)S(1)} %collective-permute-done) | copy-start | bytes 589828
  149.4 8.6 %copy-start.4 = (bf16[1024,576]{0,1:T(8,128)(2,1)S(1)}, bf16[1024,576]{0,1:T(8,128)(2,1)}, u32[]{:S(2)}) copy-start(bf16[1024,576]{0,1:T(8,128)(2,1)} %param.7) | copy-start | bytes 3538948
  164.8 28.1 %collective-permute-start.3 = (bf16[1024,96]{0,1:T(8,128)(2,1)S(1)}, bf16[1024,96]{0,1:T(8,128)(2,1)S(1)}, u32[]{:S(2)}, u32[]{:S(2)}) collective-permute-start(bf16[1024,96]{0,1:T(8,128)(2,1)S(1)} %select_convert_fusion), channel_id=1, source_target_pairs={{0,1},{1,0},{2,3},{3,2},{4,5},{5,4},{6,7},{7,6},{8,9},{9,8},{10,11... | collective-permute-start | bytes 589832 | tf_op jit(solution)/shard_map/ppermute | solution.py:12
  192.6 1.5 collective-permute-start.2
  194.2 18.8 %copy-start.2 = (bf16[9216,96]{0,1:T(8,128)(2,1)S(1)}, bf16[9216,96]{0,1:T(8,128)(2,1)}, u32[]{:S(2)}) copy-start(bf16[9216,96]{0,1:T(8,128)(2,1)} %param.8) | copy-start | bytes 5308420
  212.7 262.4 %reduce-scatter.5.cloned.1.call-start = ((), (), s32[]{:S(2)}) async-start(), calls=%async_computation.3 | async-start | bytes 20054016 | tf_op jit(solution)/shard_map/reduce_scatter | solution.py:75
  223.9 0.9 copy-start.7
  223.9 1.0 copy-start.9
  224.9 250.2 %copy-start.1 = (bf16[1024,576]{0,1:T(8,128)(2,1)S(1)}, bf16[1024,576]{0,1:T(8,128)(2,1)}, u32[]{:S(2)}) copy-start(bf16[1024,576]{0,1:T(8,128)(2,1)} %param.6) | copy-start | bytes 3538948
Sparse Core Ops, SparseCore 0:
  10.5 118.6 all-gather.1
  212.9 99.8 reduce-scatter.6
  317.7 157.4 reduce-scatter.4
where the time goes:
time: 485 us; the launch traced here: 482 us
  waiting for transfers between devices  350 us (72%)
  matrix products  105 us (22%)
  between operations  13.9 us (3%)
  local copies, waits for them, and re-layouts  9.63 us (2%)
    reduce_scatter x1, waiting for transfers between devices, body(): lax.psum_scatter(lax.dot_general(block, w_all, (((1,), (1,)), ((), ())),...  160 us
    all_gather x1, waiting for transfers between devices, body(): seq_rows = lax.all_gather(inputs, 'tensor', axis=0, tiled=True)  120 us
    unnamed x4, waiting for transfers between devices  69.3 us
    dot_general x1, matrix products, body(): jnp.einsum('hqk,qhd->kd', d_scores, queries3, preferred_element_type=jnp....  19.8 us
    dot_general x1, matrix products, body(): jnp.einsum('hqk,kd->qhd', d_scores, key_rows, preferred_element_type=jnp....  19.2 us
    dot_general x1, matrix products, body(): jnp.dot(seq_rows, w_key, preferred_element_type=jnp.float32)  12.9 us
    dot_general x1, matrix products, body(): lax.dot_general(block, d_all, (((0,), (0,)), ((), ())), preferred_element...  12.2 us
    dot_general x1, matrix products, body(): lax.dot_general(block, w_all, (((1,), (1,)), ((), ())), preferred_element...  10.9 us
  transfers between devices with their start and end apart: 7, of which 4 were waited for; matrix products, arithmetic and copies ran while one was open for 17% of the time, Pallas kernels for 0%

commit v1 on v0

v1 whole, which is shorter than its diff:
```python
import functools

import jax
import jax.numpy as jnp
from jax import lax
from jax.experimental import pallas as pl
from jax.experimental.pallas import tpu as pltpu
from jax.sharding import Mesh, PartitionSpec as P

HEAD = 192
HALF = 96
BLOCK = 64
BF = jnp.bfloat16
F32 = jnp.float32
REL = ((0, 0), (3, 0), (1, 0), (0, 1), (2, 0), (3, 1), (1, 1), (2, 1))
FLIP = (3, 5, 6, 0, 7, 1, 2, 4)


def ring(value, axis, step):
    return lax.ppermute(value, axis, [(i, (i + step) % 4) for i in range(4)])


def pair(value, axis):
    return lax.ppermute(value, axis, [(0, 1), (1, 0)])


def attn_kernel(tab, q_ref, g_ref, own_ref, oth_ref, dq_ref, down_ref, doth_ref, kt, vt, kn, dkt, dvt):
    core = tab[8]
    lo = pl.multiple_of(core * HALF, HALF)
    hi = pl.multiple_of(HALF - core * HALF, HALF)
    scale = HEAD ** -0.5
    for half, ref, a, b in ((0, own_ref, lo, hi), (1, oth_ref, hi, lo)):
        for jj in range(4):
            blk = jnp.concatenate([ref[tab[2 * jj]], ref[tab[2 * jj + 1]]], 0)
            t = blk.T
            col = slice(256 * jj + 128 * half, 256 * jj + 128 * half + 128)
            kt[pl.ds(a, HALF), col] = t[0:96]
            vt[pl.ds(a, HALF), col] = t[96:192]
            kt[pl.ds(b, HALF), col] = t[192:288]
            vt[pl.ds(b, HALF), col] = t[288:384]
    kn[...] = kt[...].T
    dkt[...] = jnp.zeros_like(dkt)
    dvt[...] = jnp.zeros_like(dvt)
    row = lax.broadcasted_iota(jnp.int32, (256, 256), 0)
    col = lax.broadcasted_iota(jnp.int32, (256, 256), 1)
    parity = jnp.where(col < 128, core, 1 - core)
    pos = ((col % 128) // 64) * 128 + parity * 64 + col % 64
    mask = row >= pos
    for i in range(4):
        width = 256 * (i + 1)
        rows = slice(256 * i, 256 * i + 256)
        dqs = []
        for j in range(3):
            q = q_ref[rows, HEAD * j:HEAD * (j + 1)]
            g = g_ref[rows, HEAD * j:HEAD * (j + 1)]
            s = jnp.dot(q, kt[:, :width], preferred_element_type=F32)
            last = jnp.where(mask, s[:, width - 256:], -jnp.inf)
            s = last if i == 0 else jnp.concatenate([s[:, :width - 256], last], 1)
            top = jnp.max(s, -1, keepdims=True)
            p = jnp.exp((s - top) * scale)
            inv = 1.0 / jnp.sum(p, -1, keepdims=True)
            dp = jnp.dot(g, vt[:, :width], preferred_element_type=F32)
            pn = p * inv
            total = jnp.sum(pn * dp, -1, keepdims=True)
            ds = (pn * ((dp - total) * scale)).astype(BF)
            low = pn.astype(BF)
            dqs.append(jnp.dot(ds, kn[:width, :], preferred_element_type=F32).astype(BF))
            dims = (((0,), (0,)), ((), ()))
            dkt[:, :width] += lax.dot_general(q, ds, dims, preferred_element_type=F32)
            dvt[:, :width] += lax.dot_general(g, low, dims, preferred_element_type=F32)
        dq_ref[rows, :] = jnp.concatenate(dqs, 1)
    for half, ref, a, b in ((0, down_ref, lo, hi), (1, doth_ref, hi, lo)):
        for jj in range(4):
            col = slice(256 * jj + 128 * half, 256 * jj + 128 * half + 128)
            t = jnp.concatenate(
                [dkt[pl.ds(a, HALF), col], dvt[pl.ds(a, HALF), col], dkt[pl.ds(b, HALF), col], dvt[pl.ds(b, HALF), col]], 0
            ).T
            ref[tab[2 * jj]] = t[:64].astype(ref.dtype)
            ref[tab[2 * jj + 1]] = t[64:].astype(ref.dtype)


def attention(table, queries, d_attn, own, oth):
    vm = pl.BlockSpec(memory_space=pltpu.VMEM)
    return pl.pallas_call(
        attn_kernel,
        in_specs=[pl.BlockSpec(memory_space=pltpu.SMEM), vm, vm, vm, vm],
        out_specs=[vm, vm, vm],
        out_shape=[
            jax.ShapeDtypeStruct(queries.shape, BF),
            jax.ShapeDtypeStruct((8, BLOCK, 2 * HEAD), F32),
            jax.ShapeDtypeStruct((8, BLOCK, 2 * HEAD), BF),
        ],
        scratch_shapes=[
            pltpu.VMEM((HEAD, 1024), BF),
            pltpu.VMEM((HEAD, 1024), BF),
            pltpu.VMEM((1024, HEAD), BF),
            pltpu.VMEM((HEAD, 1024), F32),
            pltpu.VMEM((HEAD, 1024), F32),
        ],
        compiler_params=pltpu.CompilerParams(vmem_limit_bytes=48 * 1024 * 1024),
        cost_estimate=pl.CostEstimate(flops=6 * 10**9, bytes_accessed=6 * 10**6, transcendentals=2 * 10**6),
        name="attention",
    )(table, queries, d_attn, own, oth)


def grad_kernel(place, dd_ref, x1_ref, x2_ref, keep_ref, send_ref, ddt):
    @pl.when(pl.program_id(0) == 0)
    def _():
        ddt[...] = dd_ref[...].T

    out = jnp.dot(ddt[:, :256], x1_ref[...], preferred_element_type=F32)
    out += jnp.dot(ddt[:, 256:], x2_ref[...], preferred_element_type=F32)
    out = out.astype(BF)
    keep_ref[0] = jnp.concatenate([out[0:192], out[384:576]], 0)
    send_ref[0] = jnp.concatenate([out[192:384], out[576:768]], 0)


def weight_grads(place, dd, x1, x2):
    width = x1.shape[1] // 4
    xs = pl.BlockSpec((256, width), lambda r, p: (0, (p[0] + r) % 4))
    out = pl.BlockSpec((1, 2 * HEAD, width), lambda r, p: (r, 0, 0))
    shape = jax.ShapeDtypeStruct((4, 2 * HEAD, width), BF)
    return pl.pallas_call(
        grad_kernel,
        grid_spec=pltpu.PrefetchScalarGridSpec(
            num_scalar_prefetch=1,
            grid=(4,),
            in_specs=[pl.BlockSpec((512, 4 * HEAD), lambda r, p: (0, 0)), xs, xs],
            out_specs=[out, out],
            scratch_shapes=[pltpu.VMEM((4 * HEAD, 512), BF)],
        ),
        out_shape=[shape, shape],
        compiler_params=pltpu.CompilerParams(vmem_limit_bytes=40 * 1024 * 1024),
        cost_estimate=pl.CostEstimate(flops=3624 * 10**6, bytes_accessed=13 * 10**6, transcendentals=0),
        name="weight_grads",
    )(place, dd, x1, x2)


def body(inputs, queries, d_attn, w_key, w_value):
    x, l, z, h, c = (lax.axis_index(name) for name in ("x", "l", "z", "h", "c"))
    width = inputs.shape[1] // 8

    def halves(array):
        parts = [array[:, width * i:width * (i + 1)] for i in range(8)]
        even = jnp.concatenate(parts[0::2], 1)
        odd = jnp.concatenate(parts[1::2], 1)
        return jnp.where(h == 0, even, odd), jnp.where(h == 0, odd, even)

    own, theirs = halves(inputs)
    q = pair(theirs, "h")
    a = ring(own, "z", 1)
    b = ring(own, "z", -1)
    wt = jnp.concatenate([w_key.T, w_value.T], 0)
    w_mine, w_theirs = halves(wt)
    w_partner = pair(w_theirs, "h")
    w_other = pair(w_mine, "c")
    w_partner_other = pair(w_partner, "c")
    o0 = ring(a[:32], "z", 1)
    o1 = ring(b[32:], "z", -1)
    qa = ring(q, "z", 1)
    qb = ring(q, "z", -1)
    qo0 = ring(qa[:32], "z", 1)
    qo1 = ring(qb[32:], "z", -1)
    w_all = jnp.concatenate([w_mine, w_other, w_partner, w_partner_other], 0)
    x1 = jnp.concatenate([own, a, b, q], 0)
    x2 = jnp.concatenate([o0, o1, qa, qb, qo0, qo1], 0)
    last = (((1,), (1,)), ((), ()))
    p1 = lax.dot_general(x1, w_all, last, preferred_element_type=F32)
    p2 = lax.dot_general(x2, w_all, last, preferred_element_type=F32)
    r1 = pair(p1[:, 2 * HEAD:].astype(BF), "h")
    r2 = pair(p2[:, 2 * HEAD:].astype(BF), "h")
    mine = jnp.concatenate([p1[:, :2 * HEAD], p2[:, :2 * HEAD]], 0)
    got = jnp.concatenate([r1, r2], 0).reshape(8, BLOCK, 2 * HEAD)
    got = jnp.concatenate([got[k:k + 1] for k in FLIP], 0)
    kv = (mine.reshape(8, BLOCK, 2 * HEAD) + got.astype(F32)).astype(BF)
    kv_other = pair(kv, "c")
    zz = jnp.arange(8, dtype=jnp.int32) // 2
    hh = jnp.arange(8, dtype=jnp.int32) % 2
    lookup = jnp.array([REL.index((k // 2, k % 2)) for k in range(8)], jnp.int32)
    table = jnp.concatenate([lookup[((zz - z) % 4) * 2 + (hh ^ h)], c[None].astype(jnp.int32)])
    d_query, d_own, d_oth = attention(table, queries, d_attn, kv, kv_other)
    d_oth = pair(d_oth, "c")
    dd = (d_own + d_oth.astype(F32)).astype(BF)
    dp = pair(dd, "h")
    dp = jnp.concatenate([dp[k:k + 1] for k in FLIP], 0)
    dd = jnp.concatenate([dd, dp], 2)

    def partial(first, second):
        return jnp.dot(
            jnp.concatenate([dd[first], dd[second]], 0), w_all, preferred_element_type=F32
        )

    ga = partial(7, 5).astype(BF)
    gb = partial(6, 4)
    gc = partial(2, 1)
    gd = partial(3, 0)
    up2 = ring(ga[:64], "z", 1)
    dn1 = ring(ga[64:], "z", -1)
    dn2 = ring(gb[64:].astype(BF), "z", -1)
    up1 = ring((gb[:64] + up2.astype(F32)).astype(BF), "z", 1)
    up0 = ring(gc[:64].astype(BF), "z", 1)
    dn0 = ring((gc[64:] + dn2.astype(F32)).astype(BF), "z", -1)
    cross = pair((gd[:64] + up1.astype(F32) + dn1.astype(F32)).astype(BF), "h")
    here = (gd[64:] + up0.astype(F32) + dn0.astype(F32)).astype(BF)

    def spread(even, odd):
        parts = []
        for k in range(4):
            parts += [even[:, width * k:width * (k + 1)], odd[:, width * k:width * (k + 1)]]
        return jnp.concatenate(parts, 1)

    d_input = jnp.where(h == 0, spread(here, cross), spread(cross, here))

    keep, send = weight_grads(x[None].astype(jnp.int32), dd.reshape(512, 4 * HEAD), x1, x2)
    got = pair(send, "c")
    blocks = [keep[r].astype(F32) + got[r].astype(F32) for r in range(4)]
    far = blocks[2].astype(BF)
    f0 = ring(far[:HEAD], "x", 1).astype(F32)
    f1 = ring(far[HEAD:], "x", -1).astype(F32)
    up = jnp.concatenate([blocks[1][:HEAD] + f0, blocks[1][HEAD:]], 0).astype(BF)
    down = jnp.concatenate([blocks[3][:HEAD], blocks[3][HEAD:] + f1], 0).astype(BF)
    up = ring(up, "x", 1)
    down = ring(down, "x", -1)
    total = blocks[0] + up.astype(F32) + down.astype(F32)
    same = l == h
    low = total.astype(BF)
    first = jnp.where(same, low[HEAD:], low[:HEAD])
    got1 = lax.ppermute(first, ("l", "h"), [(2, 0), (1, 3), (0, 1), (3, 2)])
    got2 = lax.ppermute(low[HEAD:], ("l", "h"), [(2, 1), (1, 2)])
    total = jnp.where(same, total[:HEAD], got2.astype(F32)) + got1.astype(F32)
    return d_input, d_query, total[:HALF].T, total[HALF:].T


def solution(mesh):
    fine = Mesh(mesh.devices.reshape(4, 2, 4, 2, 2), ("x", "l", "z", "h", "c"))
    dp, tensor = ("x", "l"), ("z", "h", "c")
    return jax.shard_map(
        body,
        mesh=fine,
        in_specs=(P(dp + tensor, None), P(dp, tensor), P(dp, tensor), P(None, tensor), P(None, tensor)),
        out_specs=(P(dp + tensor, None), P(dp, tensor), P(dp, tensor), P(dp, tensor)),
        check_vma=False,
    )
```

time: 485 us -> 260 us (0.54)
  waiting for transfers between devices: 350 us -> 155 us
  matrix products: 105 us -> 8.42 us
  starting transfers between devices: 1.6 us -> 42.1 us
  Pallas kernels: 0 us -> 17.7 us
  between operations: 13.9 us -> 1.34 us
  other arithmetic: 1.48 us -> 13.6 us
  local copies, waits for them, and re-layouts: 9.63 us -> 20.9 us
    reduce_scatter x1 -> x0, waiting for transfers between devices: 160 us -> none  [body(): lax.psum_scatter(lax.dot_general(block, w_all, (((1,), (1,)), ((), ())),...]
    ppermute x4 -> x31, waiting for transfers between devices: 1.13 us -> 155 us  [the longest x18 84.6 us: ring(): return lax.ppermute(value, axis, [(i, (i + step) % 4) for i in range(4)])]
    all_gather x1 -> x0, waiting for transfers between devices: 120 us -> none  [body(): seq_rows = lax.all_gather(inputs, 'tensor', axis=0, tiled=True)]
    dot_general x8 -> x6, matrix products: 96.1 us -> 8.42 us  [the longest x4 4.39 us: partial(): jnp.dot(jnp.concatenate([dd[first], dd[second]], 0), w_all, preferred_ele...]
    unnamed x4 -> x0, waiting for transfers between devices: 69.3 us -> none
    ppermute x4 -> x31, starting transfers between devices: 1.26 us -> 42.1 us  [the longest x18 27.9 us: ring(): return lax.ppermute(value, axis, [(i, (i + step) % 4) for i in range(4)])]
    pallas_call x0 -> x2, Pallas kernels: none -> 17.7 us  [the longest x1 11.2 us: attention(): pl.pallas_call(attn_kernel, in_specs=[pl.BlockSpec(memory_space=pltpu.SME...]
    sub x1 -> x0, matrix products: 8.57 us -> none  [body(): attention = jnp.exp(scores - row_max)]
  transfers between devices with their start and end apart: 7 -> 31, of which waited for: 4 -> 18; matrix products, arithmetic and copies ran while one was open for 17% -> 9% of each run, Pallas kernels for 0% -> 2%
where the time goes in v1:
time: 260 us; the launch traced here: 259 us
  waiting for transfers between devices  155 us (60%)
  starting transfers between devices  42.1 us (16%)
  local copies, waits for them, and re-layouts  20.9 us (8%)
  Pallas kernels  17.7 us (7%)
  other arithmetic  13.6 us (5%)
  matrix products  8.42 us (3%)
    ppermute x18, waiting for transfers between devices, ring(): return lax.ppermute(value, axis, [(i, (i + step) % 4) for i in range(4)])  84.6 us
    ppermute x11, waiting for transfers between devices, pair(): return lax.ppermute(value, axis, [(0, 1), (1, 0)])  54.9 us
    ppermute x18, starting transfers between devices, ring(): return lax.ppermute(value, axis, [(i, (i + step) % 4) for i in range(4)])  27.9 us
    ppermute x1, waiting for transfers between devices, body(): got2 = lax.ppermute(low[HEAD:], ('l', 'h'), [(2, 1), (1, 2)])  15.8 us
    unnamed x67, local copies, waits for them, and re-layouts  15.2 us
    ppermute x11, starting transfers between devices, pair(): return lax.ppermute(value, axis, [(0, 1), (1, 0)])  12.1 us
    pallas_call x1, Pallas kernels, attention(): pl.pallas_call(attn_kernel, in_specs=[pl.BlockSpec(memory_space=pltpu.SME...  11.2 us
    pallas_call x1, Pallas kernels, weight_grads(): pl.pallas_call(grad_kernel, grid_spec=pltpu.PrefetchScalarGridSpec(num_sc...  6.46 us
  transfers between devices with their start and end apart: 31, of which 18 were waited for; matrix products, arithmetic and copies ran while one was open for 9% of the time, Pallas kernels for 2%

profile of v1, /device:TPU:22, one launch (start us, length us, event | category | flops | bytes accessed | tf_op | source)
XLA Modules:
  0.0 259.4 jit_solution(12327586070615349222)
XLA Ops:
  0.6 2.5 fusion.70
  3.1 1.7 broadcast_select_fusion.3
  4.8 2.0 collective-permute-start
  7.2 0.8 broadcast_select_fusion.1
  8.5 2.3 collective-permute-start.1
  10.8 3.2 %collective-permute-start.2 = (bf16[64,4608]{1,0:T(8,128)(2,1)S(1)}, bf16[64,4608]{1,0:T(8,128)(2,1)S(1)}, u32[]{:S(2)}, u32[]{:S(2)}) collective-permute-start(bf16[64,4608]{1,0:T(8,128)(2,1)S(1)} %get-tuple-element.40), channel_id=1, source_target_pairs={{0,2},{2,0},{1,3},{3,1},{4,6},{6,4},{5,7},{7,5},{8,10},{10,8},{9,1... | collective-permute-start | bytes 1769480 | tf_op jit(solution)/shard_map/ppermute | solution.py:24
  14.0 8.3 %collective-permute-done = bf16[64,4608]{1,0:T(8,128)(2,1)S(1)} collective-permute-done((bf16[64,4608]{1,0:T(8,128)(2,1)S(1)}, bf16[64,4608]{1,0:T(8,128)(2,1)S(1)}, u32[]{:S(2)}, u32[]{:S(2)}) %collective-permute-start) | collective-permute-done | bytes 589856 | tf_op jit(solution)/shard_map/ppermute | solution.py:20
  23.2 3.7 %collective-permute-start.7 = (bf16[32,4608]{1,0:T(8,128)(2,1)S(1)}, bf16[32,4608]{1,0:T(8,128)(2,1)S(1)}, u32[]{:S(2)}, u32[]{:S(2)}) collective-permute-start(bf16[32,4608]{1,0:T(8,128)(2,1)S(1)} %slice.425), channel_id=1, source_target_pairs={{0,12},{4,0},{8,4},{12,8},{1,13},{5,1},{9,5},{13,9},{2,14},{6,2},{... | collective-permute-start | bytes 884744 | tf_op jit(solution)/shard_map/ppermute | solution.py:20
  26.9 35.4 %collective-permute-done.2 = bf16[64,4608]{1,0:T(8,128)(2,1)S(1)} collective-permute-done((bf16[64,4608]{1,0:T(8,128)(2,1)S(1)}, bf16[64,4608]{1,0:T(8,128)(2,1)S(1)}, u32[]{:S(2)}, u32[]{:S(2)}) %collective-permute-start.2) | collective-permute-done | bytes 589856 | tf_op jit(solution)/shard_map/ppermute | solution.py:24
  62.3 1.9 collective-permute-start.8
  64.3 1.3 collective-permute-start.9
  65.6 11.8 %collective-permute-done.8 = bf16[64,4608]{1,0:T(8,128)(2,1)S(1)} collective-permute-done((bf16[64,4608]{1,0:T(8,128)(2,1)S(1)}, bf16[64,4608]{1,0:T(8,128)(2,1)S(1)}, u32[]{:S(2)}, u32[]{:S(2)}) %collective-permute-start.8) | collective-permute-done | bytes 589856 | tf_op jit(solution)/shard_map/ppermute | solution.py:20
  77.4 0.8 collective-permute-start.10
  78.3 2.6 %collective-permute-start.11 = (bf16[32,4608]{1,0:T(8,128)(2,1)S(1)}, bf16[32,4608]{1,0:T(8,128)(2,1)S(1)}, u32[]{:S(2)}, u32[]{:S(2)}) collective-permute-start(bf16[32,4608]{1,0:T(8,128)(2,1)S(1)} %slice.427), channel_id=1, source_target_pairs={{0,12},{4,0},{8,4},{12,8},{1,13},{5,1},{9,5},{13,9},{2,14},{6,2},{... | collective-permute-start | bytes 884744 | tf_op jit(solution)/shard_map/ppermute | solution.py:20
  80.9 4.5 %collective-permute-done.10 = bf16[32,4608]{1,0:T(8,128)(2,1)S(1)} collective-permute-done((bf16[32,4608]{1,0:T(8,128)(2,1)S(1)}, bf16[32,4608]{1,0:T(8,128)(2,1)S(1)}, u32[]{:S(2)}, u32[]{:S(2)}) %collective-permute-start.10) | collective-permute-done | bytes 294944 | tf_op jit(solution)/shard_map/ppermute | solution.py:20
  86.2 2.0 fusion.66
  89.1 2.0 fusion.72
  91.2 2.9 %collective-permute-start.13 = (bf16[256,384]{1,0:T(8,128)(2,1)S(1)}, bf16[256,384]{1,0:T(8,128)(2,1)S(1)}, u32[]{:S(2)}, u32[]{:S(2)}) collective-permute-start(bf16[256,384]{1,0:T(8,128)(2,1)S(1)} %slice.715), channel_id=1, source_target_pairs={{0,2},{2,0},{1,3},{3,1},{4,6},{6,4},{5,7},{7,5},{8,10},{10,8},{9,1... | collective-permute-start | bytes 589832 | tf_op jit(solution)/shard_map/ppermute | solution.py:24
  94.2 2.9 %collective-permute-done.12 = bf16[256,384]{1,0:T(8,128)(2,1)S(1)} collective-permute-done((bf16[256,384]{1,0:T(8,128)(2,1)S(1)}, bf16[256,384]{1,0:T(8,128)(2,1)S(1)}, u32[]{:S(2)}, u32[]{:S(2)}) %collective-permute-start.12) | collective-permute-done | bytes 196640 | tf_op jit(solution)/shard_map/ppermute | solution.py:24
  97.1 2.9 %collective-permute-done.13 = bf16[256,384]{1,0:T(8,128)(2,1)S(1)} collective-permute-done((bf16[256,384]{1,0:T(8,128)(2,1)S(1)}, bf16[256,384]{1,0:T(8,128)(2,1)S(1)}, u32[]{:S(2)}, u32[]{:S(2)}) %collective-permute-start.13) | collective-permute-done | bytes 196640 | tf_op jit(solution)/shard_map/ppermute | solution.py:24
  101.2 1.7 copy.14.g_ref
  103.7 0.8 copy-done.5
  104.5 1.0 copy-done.2
  105.5 1.0 copy-done.6
  106.5 11.2 %attention.1 = (bf16[1024,576]{1,0:T(8,128)(2,1)S(1)}, f32[8,64,384]{2,1,0:T(8,128)S(1)}, bf16[8,64,384]{2,1,0:T(8,128)(2,1)}) custom-call(s32[9]{0:T(128)S(1)} %pad_add_fusion.tab, bf16[1024,576]{1,0:T(8,128)(2,1)S(1)} %copy.13.q_ref, bf16[1024,576]{1,0:T(8,128)(2,1)S(1)} %copy.14.g_ref, bf16[8,64,384]{2,1,0:T(8,128)(2,1)S(1)} %copy-done.2, ...), custom_call_target="tpu_custom_call" | custom-call | flops 6000000000 | bytes 6000000 | tf_op jit(solution)/shard_map/attention/pallas_call | solution.py:84
  117.7 1.1 copy-done
  119.3 1.6 collective-permute-done.15
  120.9 1.6 collective-permute-start.16
  122.5 2.4 pad_maximum_fusion.1.x1_ref
  124.9 9.2 %collective-permute-done.16 = bf16[8,64,384]{2,1,0:T(8,128)(2,1)S(1)} collective-permute-done((bf16[8,64,384]{2,1,0:T(8,128)(2,1)S(1)}, bf16[8,64,384]{2,1,0:T(8,128)(2,1)S(1)}, u32[]{:S(2)}, u32[]{:S(2)}) %collective-permute-start.16) | collective-permute-done | bytes 393248 | tf_op jit(solution)/shard_map/ppermute | solution.py:24
  134.3 1.1 fusion.33
  135.5 1.8 collective-permute-start.18
  137.3 1.1 fusion.29
  138.8 1.1 convolution_convert_fusion
  140.3 3.0 %collective-permute-start.22 = (bf16[64,4608]{1,0:T(8,128)(2,1)S(1)}, bf16[64,4608]{1,0:T(8,128)(2,1)S(1)}, u32[]{:S(2)}, u32[]{:S(2)}) collective-permute-start(bf16[64,4608]{1,0:T(8,128)(2,1)S(1)} %get-tuple-element.39), channel_id=1, source_target_pairs={{0,12},{4,0},{8,4},{12,8},{1,13},{5,1},{9,5},{13,9},{2,14},{6,2},{... | collective-permute-start | bytes 1769480 | tf_op jit(solution)/shard_map/ppermute | solution.py:20
  143.3 8.5 %collective-permute-done.18 = bf16[64,4608]{1,0:T(8,128)(2,1)S(1)} collective-permute-done((bf16[64,4608]{1,0:T(8,128)(2,1)S(1)}, bf16[64,4608]{1,0:T(8,128)(2,1)S(1)}, u32[]{:S(2)}, u32[]{:S(2)}) %collective-permute-start.18) | collective-permute-done | bytes 589856 | tf_op jit(solution)/shard_map/ppermute | solution.py:20
  151.9 3.1 %collective-permute-start.19 = (bf16[64,4608]{1,0:T(8,128)(2,1)S(1)}, bf16[64,4608]{1,0:T(8,128)(2,1)S(1)}, u32[]{:S(2)}, u32[]{:S(2)}) collective-permute-start(bf16[64,4608]{1,0:T(8,128)(2,1)S(1)} %fusion.8), channel_id=1, source_target_pairs={{0,12},{4,0},{8,4},{12,8},{1,13},{5,1},{9,5},{13,9},{2,14},{6,2},{... | collective-permute-start | bytes 1769480 | tf_op jit(solution)/shard_map/ppermute | solution.py:20
  155.0 12.0 %collective-permute-done.20 = bf16[64,4608]{1,0:T(8,128)(2,1)S(1)} collective-permute-done((bf16[64,4608]{1,0:T(8,128)(2,1)S(1)}, bf16[64,4608]{1,0:T(8,128)(2,1)S(1)}, u32[]{:S(2)}, u32[]{:S(2)}) %collective-permute-start.20) | collective-permute-done | bytes 589856 | tf_op jit(solution)/shard_map/ppermute | solution.py:20
  167.2 1.1 fusion.25
  168.3 7.3 %collective-permute-done.19 = bf16[64,4608]{1,0:T(8,128)(2,1)S(1)} collective-permute-done((bf16[64,4608]{1,0:T(8,128)(2,1)S(1)}, bf16[64,4608]{1,0:T(8,128)(2,1)S(1)}, u32[]{:S(2)}, u32[]{:S(2)}) %collective-permute-start.19) | collective-permute-done | bytes 589856 | tf_op jit(solution)/shard_map/ppermute | solution.py:20
  175.6 6.3 %collective-permute-done.21 = bf16[64,4608]{1,0:T(8,128)(2,1)S(1)} collective-permute-done((bf16[64,4608]{1,0:T(8,128)(2,1)S(1)}, bf16[64,4608]{1,0:T(8,128)(2,1)S(1)}, u32[]{:S(2)}, u32[]{:S(2)}) %collective-permute-start.21) | collective-permute-done | bytes 589856 | tf_op jit(solution)/shard_map/ppermute | solution.py:20
  181.9 1.5 fusion.7
  183.4 2.8 %collective-permute-start.23 = (bf16[64,4608]{1,0:T(8,128)(2,1)}, bf16[64,4608]{1,0:T(8,128)(2,1)}, u32[]{:S(2)}, u32[]{:S(2)}) collective-permute-start(bf16[64,4608]{1,0:T(8,128)(2,1)} %get-tuple-element.36), channel_id=1, source_target_pairs={{0,2},{2,0},{1,3},{3,1},{4,6},{6,4},{5,7},{7,5},{8,10},{10,8},{9,1... | collective-permute-start | bytes 1769480 | tf_op jit(solution)/shard_map/ppermute | solution.py:24
  186.2 6.5 %weight_grads.1 = (bf16[4,384,1152]{2,1,0:T(8,128)(2,1)S(1)}, bf16[4,384,1152]{2,1,0:T(8,128)(2,1)}) custom-call(s32[1]{0:T(128)} %bitcast.21.place, bf16[512,768]{1,0:T(8,128)(2,1)S(1)} %bitcast.92, bf16[256,4608]{1,0:T(8,128)(2,1)S(1)} %pad_maximum_fusion.1.x1_ref, bf16[256,4608]{1,0:T(8,128)(2,1)S(1)} %copy-done.4), custom_call_target="tpu_custom_call" | custom-call | flops 3624000000 | bytes 13000000 | tf_op jit(solution)/shard_map/weight_grads/pallas_call | solution.py:123
  192.7 2.4 copy.15
  195.0 2.9 %collective-permute-done.23 = bf16[64,4608]{1,0:T(8,128)(2,1)} collective-permute-done((bf16[64,4608]{1,0:T(8,128)(2,1)}, bf16[64,4608]{1,0:T(8,128)(2,1)}, u32[]{:S(2)}, u32[]{:S(2)}) %collective-permute-start.23) | collective-permute-done | bytes 589856 | tf_op jit(solution)/shard_map/ppermute | solution.py:24
  197.9 0.9 slice_dynamic-update-slice_fusion.12
  198.8 0.9 slice_dynamic-update-slice_fusion.14
  199.8 1.0 slice_dynamic-update-slice_fusion.8
  200.8 0.9 slice_dynamic-update-slice_fusion.10
  201.7 1.0 slice_dynamic-update-slice_fusion.4
  202.8 1.0 slice_dynamic-update-slice_fusion
  203.8 2.2 convert_add_fusion.1
  206.8 1.9 collective-permute-start.27
  208.7 7.6 %collective-permute-done.25 = bf16[192,1152]{1,0:T(8,128)(2,1)S(1)} collective-permute-done((bf16[192,1152]{1,0:T(8,128)(2,1)S(1)}, bf16[192,1152]{1,0:T(8,128)(2,1)S(1)}, u32[]{:S(2)}, u32[]{:S(2)}) %collective-permute-start.25) | collective-permute-done | bytes 442400 | tf_op jit(solution)/shard_map/ppermute | solution.py:20
  216.5 1.5 collective-permute-start.26
  218.9 0.9 slice_dynamic-update-slice_fusion.1
  219.8 15.2 %collective-permute-done.26 = bf16[384,1152]{1,0:T(8,128)(2,1)S(1)} collective-permute-done((bf16[384,1152]{1,0:T(8,128)(2,1)S(1)}, bf16[384,1152]{1,0:T(8,128)(2,1)S(1)}, u32[]{:S(2)}, u32[]{:S(2)}) %collective-permute-start.26) | collective-permute-done | bytes 884768 | tf_op jit(solution)/shard_map/ppermute | solution.py:20
  235.0 2.5 collective-permute-done.28
  237.5 1.6 fusion.67
  239.2 2.0 collective-permute-start.29
  241.3 1.1 broadcast_select_fusion.2
  242.4 15.8 %collective-permute-done.29 = bf16[192,1152]{1,0:T(8,128)(2,1)S(1)} collective-permute-done((bf16[192,1152]{1,0:T(8,128)(2,1)S(1)}, bf16[192,1152]{1,0:T(8,128)(2,1)S(1)}, u32[]{:S(2)}, u32[]{:S(2)}) %collective-permute-start.29) | collective-permute-done | bytes 442400 | tf_op jit(solution)/shard_map/ppermute | solution.py:229
  258.4 1.0 slice_bitcast_fusion.2
  (120 shorter events, 9.6 us)
Async XLA Ops:
  0.6 6.1 %copy-start.11 = (bf16[9216,96]{0,1:T(8,128)(2,1)S(1)}, bf16[9216,96]{0,1:T(8,128)(2,1)}, u32[]{:S(2)}) copy-start(bf16[9216,96]{0,1:T(8,128)(2,1)} %param.10) | copy-start | bytes 5308420
  3.1 3.7 %copy-start.10 = (bf16[9216,96]{0,1:T(8,128)(2,1)S(1)}, bf16[9216,96]{0,1:T(8,128)(2,1)}, u32[]{:S(2)}) copy-start(bf16[9216,96]{0,1:T(8,128)(2,1)} %param.9) | copy-start | bytes 5308420
  4.8 81.4 %copy-start.12 = (bf16[64,4608]{1,0:T(8,128)(2,1)}, bf16[64,4608]{1,0:T(8,128)(2,1)S(1)}, u32[]{:S(2)}) copy-start(bf16[64,4608]{1,0:T(8,128)(2,1)S(1)} %get-tuple-element.41) | copy-start | bytes 1769476
  4.8 17.4 %collective-permute-start = (bf16[64,4608]{1,0:T(8,128)(2,1)S(1)}, bf16[64,4608]{1,0:T(8,128)(2,1)S(1)}, u32[]{:S(2)}, u32[]{:S(2)}) collective-permute-start(bf16[64,4608]{1,0:T(8,128)(2,1)S(1)} %get-tuple-element.41), channel_id=1, source_target_pairs={{0,4},{4,8},{8,12},{12,0},{1,5},{5,9},{9,13},{13,1},{2,6},{6,10},{... | collective-permute-start | bytes 1769480 | tf_op jit(solution)/shard_map/ppermute | solution.py:20
  8.0 72.8 %collective-permute-start.4 = (bf16[192,4608]{1,0:T(8,128)(2,1)S(1)}, bf16[192,4608]{1,0:T(8,128)(2,1)S(1)}, u32[]{:S(2)}, u32[]{:S(2)}) collective-permute-start(bf16[192,4608]{1,0:T(8,128)(2,1)S(1)} %get-tuple-element.28), channel_id=1, source_target_pairs={{0,2},{2,0},{1,3},{3,1},{4,6},{6,4},{5,7},{7,5},{8,10},{10,8},{9,1... | collective-permute-start | bytes 5308424 | tf_op jit(solution)/shard_map/ppermute | solution.py:24
  8.5 14.7 %collective-permute-start.1 = (bf16[64,4608]{1,0:T(8,128)(2,1)S(1)}, bf16[64,4608]{1,0:T(8,128)(2,1)S(1)}, u32[]{:S(2)}, u32[]{:S(2)}) collective-permute-start(bf16[64,4608]{1,0:T(8,128)(2,1)S(1)} %get-tuple-element.41), channel_id=1, source_target_pairs={{0,12},{4,0},{8,4},{12,8},{1,13},{5,1},{9,5},{13,9},{2,14},{6,2},{... | collective-permute-start | bytes 1769480 | tf_op jit(solution)/shard_map/ppermute | solution.py:20
  10.8 51.6 %collective-permute-start.2 = (bf16[64,4608]{1,0:T(8,128)(2,1)S(1)}, bf16[64,4608]{1,0:T(8,128)(2,1)S(1)}, u32[]{:S(2)}, u32[]{:S(2)}) collective-permute-start(bf16[64,4608]{1,0:T(8,128)(2,1)S(1)} %get-tuple-element.40), channel_id=1, source_target_pairs={{0,2},{2,0},{1,3},{3,1},{4,6},{6,4},{5,7},{7,5},{8,10},{10,8},{9,1... | collective-permute-start | bytes 1769480 | tf_op jit(solution)/shard_map/ppermute | solution.py:24
  22.2 64.0 %copy-start.15 = (bf16[64,4608]{1,0:T(8,128)(2,1)}, bf16[64,4608]{1,0:T(8,128)(2,1)S(1)}, u32[]{:S(2)}) copy-start(bf16[64,4608]{1,0:T(8,128)(2,1)S(1)} %collective-permute-done) | copy-start | bytes 1769476
  22.2 42.0 %collective-permute-start.6 = (bf16[32,4608]{1,0:T(8,128)(2,1)S(1)}, bf16[32,4608]{1,0:T(8,128)(2,1)S(1)}, u32[]{:S(2)}, u32[]{:S(2)}) collective-permute-start(bf16[32,4608]{1,0:T(8,128)(2,1)S(1)} %slice.424), channel_id=1, source_target_pairs={{0,4},{4,8},{8,12},{12,0},{1,5},{5,9},{9,13},{13,1},{2,6},{6,10},{... | collective-permute-start | bytes 884744 | tf_op jit(solution)/shard_map/ppermute | solution.py:20
  22.3 63.2 %collective-permute-start.3 = (bf16[192,4608]{1,0:T(8,128)(2,1)S(1)}, bf16[192,4608]{1,0:T(8,128)(2,1)S(1)}, u32[]{:S(2)}, u32[]{:S(2)}) collective-permute-start(bf16[192,4608]{1,0:T(8,128)(2,1)S(1)} %get-tuple-element.27), channel_id=1, source_target_pairs={{0,1},{1,0},{2,3},{3,2},{4,5},{5,4},{6,7},{7,6},{8,9},{9,8},{10,11... | collective-permute-start | bytes 5308424 | tf_op jit(solution)/shard_map/ppermute | solution.py:24
  23.2 63.0 %copy-start.17 = (bf16[64,4608]{1,0:T(8,128)(2,1)}, bf16[64,4608]{1,0:T(8,128)(2,1)S(1)}, u32[]{:S(2)}) copy-start(bf16[64,4608]{1,0:T(8,128)(2,1)S(1)} %collective-permute-done.1) | copy-start | bytes 1769476
  23.2 42.4 %collective-permute-start.7 = (bf16[32,4608]{1,0:T(8,128)(2,1)S(1)}, bf16[32,4608]{1,0:T(8,128)(2,1)S(1)}, u32[]{:S(2)}, u32[]{:S(2)}) collective-permute-start(bf16[32,4608]{1,0:T(8,128)(2,1)S(1)} %slice.425), channel_id=1, source_target_pairs={{0,12},{4,0},{8,4},{12,8},{1,13},{5,1},{9,5},{13,9},{2,14},{6,2},{... | collective-permute-start | bytes 884744 | tf_op jit(solution)/shard_map/ppermute | solution.py:20
  62.3 23.9 %copy-start.19 = (bf16[64,4608]{1,0:T(8,128)(2,1)}, bf16[64,4608]{1,0:T(8,128)(2,1)S(1)}, u32[]{:S(2)}) copy-start(bf16[64,4608]{1,0:T(8,128)(2,1)S(1)} %collective-permute-done.2) | copy-start | bytes 1769476
  62.3 15.1 %collective-permute-start.8 = (bf16[64,4608]{1,0:T(8,128)(2,1)S(1)}, bf16[64,4608]{1,0:T(8,128)(2,1)S(1)}, u32[]{:S(2)}, u32[]{:S(2)}) collective-permute-start(bf16[64,4608]{1,0:T(8,128)(2,1)S(1)} %collective-permute-done.2), channel_id=1, source_target_pairs={{0,4},{4,8},{8,12},{12,0},{1,5},{5,9},{9,13},{13,1},{2,6},{6,10},{... | collective-permute-start | bytes 1769480 | tf_op jit(solution)/shard_map/ppermute | solution.py:20
  64.3 14.0 %collective-permute-start.9 = (bf16[64,4608]{1,0:T(8,128)(2,1)S(1)}, bf16[64,4608]{1,0:T(8,128)(2,1)S(1)}, u32[]{:S(2)}, u32[]{:S(2)}) collective-permute-start(bf16[64,4608]{1,0:T(8,128)(2,1)S(1)} %collective-permute-done.2), channel_id=1, source_target_pairs={{0,12},{4,0},{8,4},{12,8},{1,13},{5,1},{9,5},{13,9},{2,14},{6,2},{... | collective-permute-start | bytes 1769480 | tf_op jit(solution)/shard_map/ppermute | solution.py:20
  77.4 8.0 %collective-permute-start.10 = (bf16[32,4608]{1,0:T(8,128)(2,1)S(1)}, bf16[32,4608]{1,0:T(8,128)(2,1)S(1)}, u32[]{:S(2)}, u32[]{:S(2)}) collective-permute-start(bf16[32,4608]{1,0:T(8,128)(2,1)S(1)} %slice.426), channel_id=1, source_target_pairs={{0,4},{4,8},{8,12},{12,0},{1,5},{5,9},{9,13},{13,1},{2,6},{6,10},{... | collective-permute-start | bytes 884744 | tf_op jit(solution)/shard_map/ppermute | solution.py:20
  78.3 7.2 %collective-permute-start.11 = (bf16[32,4608]{1,0:T(8,128)(2,1)S(1)}, bf16[32,4608]{1,0:T(8,128)(2,1)S(1)}, u32[]{:S(2)}, u32[]{:S(2)}) collective-permute-start(bf16[32,4608]{1,0:T(8,128)(2,1)S(1)} %slice.427), channel_id=1, source_target_pairs={{0,12},{4,0},{8,4},{12,8},{1,13},{5,1},{9,5},{13,9},{2,14},{6,2},{... | collective-permute-start | bytes 884744 | tf_op jit(solution)/shard_map/ppermute | solution.py:20
  80.9 4.7 %collective-permute-start.5 = (bf16[192,4608]{1,0:T(8,128)(2,1)S(1)}, bf16[192,4608]{1,0:T(8,128)(2,1)S(1)}, u32[]{:S(2)}, u32[]{:S(2)}) collective-permute-start(bf16[192,4608]{1,0:T(8,128)(2,1)S(1)} %collective-permute-done.4), channel_id=1, source_target_pairs={{0,1},{1,0},{2,3},{3,2},{4,5},{5,4},{6,7},{7,6},{8,9},{9,8},{10,11... | collective-permute-start | bytes 5308424 | tf_op jit(solution)/shard_map/ppermute | solution.py:24
  85.5 3.2 %copy-start.3 = (bf16[256,4608]{1,0:T(8,128)(2,1)}, bf16[256,4608]{1,0:T(8,128)(2,1)S(1)}, u32[]{:S(2)}) copy-start(bf16[256,4608]{1,0:T(8,128)(2,1)S(1)} %constant_dynamic-update-slice_fusion.x2_ref) | copy-start | bytes 7077892
  86.2 2.9 %copy-start.8 = (bf16[768,4608]{1,0:T(8,128)(2,1)}, bf16[768,4608]{1,0:T(8,128)(2,1)S(1)}, u32[]{:S(2)}) copy-start(bf16[768,4608]{1,0:T(8,128)(2,1)S(1)} %pad_maximum_fusion) | copy-start | bytes 21233668
  88.3 8.8 %collective-permute-start.12 = (bf16[256,384]{1,0:T(8,128)(2,1)S(1)}, bf16[256,384]{1,0:T(8,128)(2,1)S(1)}, u32[]{:S(2)}, u32[]{:S(2)}) collective-permute-start(bf16[256,384]{1,0:T(8,128)(2,1)S(1)} %slice.716), channel_id=1, source_target_pairs={{0,2},{2,0},{1,3},{3,1},{4,6},{6,4},{5,7},{7,5},{8,10},{10,8},{9,1... | collective-permute-start | bytes 589832 | tf_op jit(solution)/shard_map/ppermute | solution.py:24
  91.2 9.3 %copy-start.18 = (bf16[1024,576]{0,1:T(8,128)(2,1)S(1)}, bf16[1024,576]{0,1:T(8,128)(2,1)}, u32[]{:S(2)}) copy-start(bf16[1024,576]{0,1:T(8,128)(2,1)} %param.7) | copy-start | bytes 3538948
  91.2 8.8 %collective-permute-start.13 = (bf16[256,384]{1,0:T(8,128)(2,1)S(1)}, bf16[256,384]{1,0:T(8,128)(2,1)S(1)}, u32[]{:S(2)}, u32[]{:S(2)}) collective-permute-start(bf16[256,384]{1,0:T(8,128)(2,1)S(1)} %slice.715), channel_id=1, source_target_pairs={{0,2},{2,0},{1,3},{3,1},{4,6},{6,4},{5,7},{7,5},{8,10},{10,8},{9,1... | collective-permute-start | bytes 589832 | tf_op jit(solution)/shard_map/ppermute | solution.py:24
  100.2 2.7 %copy-start.1 = (bf16[8,64,384]{2,1,0:T(8,128)(2,1)}, bf16[8,64,384]{2,1,0:T(8,128)(2,1)S(1)}, u32[]{:S(2)}) copy-start(bf16[8,64,384]{2,1,0:T(8,128)(2,1)S(1)} %add_convert_fusion.2.own_ref) | copy-start | bytes 1179652
  100.2 3.5 %collective-permute-start.14 = (bf16[8,64,384]{2,1,0:T(8,128)(2,1)S(1)}, bf16[8,64,384]{2,1,0:T(8,128)(2,1)S(1)}, u32[]{:S(2)}, u32[]{:S(2)}) collective-permute-start(bf16[8,64,384]{2,1,0:T(8,128)(2,1)S(1)} %add_convert_fusion.2.own_ref), channel_id=1, source_target_pairs={{0,1},{1,0},{2,3},{3,2},{4,5},{5,4},{6,7},{7,6},{8,9},{9,8},{10,11... | collective-permute-start | bytes 1179656 | tf_op jit(solution)/shard_map/ppermute | solution.py:24
  101.2 1.8 copy-start.7
  103.7 0.8 copy-start.5
  104.5 1.0 copy-start.2
  105.5 1.0 copy-start.6
  117.7 1.1 copy-start
  118.8 3.7 %copy-start.13 = (bf16[64,4608]{1,0:T(8,128)(2,1)S(1)}, bf16[64,4608]{1,0:T(8,128)(2,1)}, u32[]{:S(2)}) copy-start(bf16[64,4608]{1,0:T(8,128)(2,1)} %copy-done.12) | copy-start | bytes 1769476
  118.8 3.7 %copy-start.16 = (bf16[64,4608]{1,0:T(8,128)(2,1)S(1)}, bf16[64,4608]{1,0:T(8,128)(2,1)}, u32[]{:S(2)}) copy-start(bf16[64,4608]{1,0:T(8,128)(2,1)} %copy-done.15) | copy-start | bytes 1769476
  118.8 2.0 collective-permute-start.15
  120.9 13.2 %collective-permute-start.16 = (bf16[8,64,384]{2,1,0:T(8,128)(2,1)S(1)}, bf16[8,64,384]{2,1,0:T(8,128)(2,1)S(1)}, u32[]{:S(2)}, u32[]{:S(2)}) collective-permute-start(bf16[8,64,384]{2,1,0:T(8,128)(2,1)S(1)} %add_convert_fusion.1), channel_id=1, source_target_pairs={{0,2},{2,0},{1,3},{3,1},{4,6},{6,4},{5,7},{7,5},{8,10},{10,8},{9,1... | collective-permute-start | bytes 1179656 | tf_op jit(solution)/shard_map/ppermute | solution.py:24
  122.5 11.8 %copy-start.9 = (bf16[768,4608]{1,0:T(8,128)(2,1)S(1)}, bf16[768,4608]{1,0:T(8,128)(2,1)}, u32[]{:S(2)}) copy-start(bf16[768,4608]{1,0:T(8,128)(2,1)} %copy-done.8) | copy-start | bytes 21233668
  135.5 16.3 %collective-permute-start.18 = (bf16[64,4608]{1,0:T(8,128)(2,1)S(1)}, bf16[64,4608]{1,0:T(8,128)(2,1)S(1)}, u32[]{:S(2)}, u32[]{:S(2)}) collective-permute-start(bf16[64,4608]{1,0:T(8,128)(2,1)S(1)} %slice.713), channel_id=1, source_target_pairs={{0,12},{4,0},{8,4},{12,8},{1,13},{5,1},{9,5},{13,9},{2,14},{6,2},{... | collective-permute-start | bytes 1769480 | tf_op jit(solution)/shard_map/ppermute | solution.py:20
  138.5 29.8 %collective-permute-start.17 = (bf16[64,4608]{1,0:T(8,128)(2,1)S(1)}, bf16[64,4608]{1,0:T(8,128)(2,1)S(1)}, u32[]{:S(2)}, u32[]{:S(2)}) collective-permute-start(bf16[64,4608]{1,0:T(8,128)(2,1)S(1)} %slice.714), channel_id=1, source_target_pairs={{0,4},{4,8},{8,12},{12,0},{1,5},{5,9},{9,13},{13,1},{2,6},{6,10},{... | collective-permute-start | bytes 1769480 | tf_op jit(solution)/shard_map/ppermute | solution.py:20
  140.0 26.9 %collective-permute-start.20 = (bf16[64,4608]{1,0:T(8,128)(2,1)S(1)}, bf16[64,4608]{1,0:T(8,128)(2,1)S(1)}, u32[]{:S(2)}, u32[]{:S(2)}) collective-permute-start(bf16[64,4608]{1,0:T(8,128)(2,1)S(1)} %get-tuple-element.38), channel_id=1, source_target_pairs={{0,4},{4,8},{8,12},{12,0},{1,5},{5,9},{9,13},{13,1},{2,6},{6,10},{... | collective-permute-start | bytes 1769480 | tf_op jit(solution)/shard_map/ppermute | solution.py:20
  140.3 28.0 %collective-permute-start.22 = (bf16[64,4608]{1,0:T(8,128)(2,1)S(1)}, bf16[64,4608]{1,0:T(8,128)(2,1)S(1)}, u32[]{:S(2)}, u32[]{:S(2)}) collective-permute-start(bf16[64,4608]{1,0:T(8,128)(2,1)S(1)} %get-tuple-element.39), channel_id=1, source_target_pairs={{0,12},{4,0},{8,4},{12,8},{1,13},{5,1},{9,5},{13,9},{2,14},{6,2},{... | collective-permute-start | bytes 1769480 | tf_op jit(solution)/shard_map/ppermute | solution.py:20
  151.9 23.7 %collective-permute-start.19 = (bf16[64,4608]{1,0:T(8,128)(2,1)S(1)}, bf16[64,4608]{1,0:T(8,128)(2,1)S(1)}, u32[]{:S(2)}, u32[]{:S(2)}) collective-permute-start(bf16[64,4608]{1,0:T(8,128)(2,1)S(1)} %fusion.8), channel_id=1, source_target_pairs={{0,12},{4,0},{8,4},{12,8},{1,13},{5,1},{9,5},{13,9},{2,14},{6,2},{... | collective-permute-start | bytes 1769480 | tf_op jit(solution)/shard_map/ppermute | solution.py:20
  167.0 14.9 %collective-permute-start.21 = (bf16[64,4608]{1,0:T(8,128)(2,1)S(1)}, bf16[64,4608]{1,0:T(8,128)(2,1)S(1)}, u32[]{:S(2)}, u32[]{:S(2)}) collective-permute-start(bf16[64,4608]{1,0:T(8,128)(2,1)S(1)} %fusion.5), channel_id=1, source_target_pairs={{0,4},{4,8},{8,12},{12,0},{1,5},{5,9},{9,13},{13,1},{2,6},{6,10},{... | collective-permute-start | bytes 1769480 | tf_op jit(solution)/shard_map/ppermute | solution.py:20
  168.3 17.9 %copy-start.4 = (bf16[256,4608]{1,0:T(8,128)(2,1)S(1)}, bf16[256,4608]{1,0:T(8,128)(2,1)}, u32[]{:S(2)}) copy-start(bf16[256,4608]{1,0:T(8,128)(2,1)} %copy-done.3) | copy-start | bytes 7077892
  183.4 14.5 %collective-permute-start.23 = (bf16[64,4608]{1,0:T(8,128)(2,1)}, bf16[64,4608]{1,0:T(8,128)(2,1)}, u32[]{:S(2)}, u32[]{:S(2)}) collective-permute-start(bf16[64,4608]{1,0:T(8,128)(2,1)} %get-tuple-element.36), channel_id=1, source_target_pairs={{0,2},{2,0},{1,3},{3,1},{4,6},{6,4},{5,7},{7,5},{8,10},{10,8},{9,1... | collective-permute-start | bytes 1769480 | tf_op jit(solution)/shard_map/ppermute | solution.py:24
  192.6 11.2 %collective-permute-start.24 = (bf16[4,384,1152]{2,1,0:T(8,128)(2,1)}, bf16[4,384,1152]{2,1,0:T(8,128)(2,1)}, u32[]{:S(2)}, u32[]{:S(2)}) collective-permute-start(bf16[4,384,1152]{2,1,0:T(8,128)(2,1)} %get-tuple-element.13), channel_id=1, source_target_pairs={{0,1},{1,0},{2,3},{3,2},{4,5},{5,4},{6,7},{7,6},{8,9},{9,8},{10,11... | collective-permute-start | bytes 10616840 | tf_op jit(solution)/shard_map/ppermute | solution.py:24
  195.0 7.7 %copy-start.14 = (bf16[64,4608]{1,0:T(8,128)(2,1)S(1)}, bf16[64,4608]{1,0:T(8,128)(2,1)}, u32[]{:S(2)}) copy-start(bf16[64,4608]{1,0:T(8,128)(2,1)} %get-tuple-element.37) | copy-start | bytes 1769476
  206.2 10.2 %collective-permute-start.25 = (bf16[192,1152]{1,0:T(8,128)(2,1)S(1)}, bf16[192,1152]{1,0:T(8,128)(2,1)S(1)}, u32[]{:S(2)}, u32[]{:S(2)}) collective-permute-start(bf16[192,1152]{1,0:T(8,128)(2,1)S(1)} %get-tuple-element.54), channel_id=1, source_target_pairs={{0,32},{32,64},{64,96},{96,0},{1,33},{33,65},{65,97},{97,1},{2,34}... | collective-permute-start | bytes 1327112 | tf_op jit(solution)/shard_map/ppermute | solution.py:20
  206.8 11.2 %collective-permute-start.27 = (bf16[192,1152]{1,0:T(8,128)(2,1)S(1)}, bf16[192,1152]{1,0:T(8,128)(2,1)S(1)}, u32[]{:S(2)}, u32[]{:S(2)}) collective-permute-start(bf16[192,1152]{1,0:T(8,128)(2,1)S(1)} %get-tuple-element.55), channel_id=1, source_target_pairs={{0,96},{32,0},{64,32},{96,64},{1,97},{33,1},{65,33},{97,65},{2,98}... | collective-permute-start | bytes 1327112 | tf_op jit(solution)/shard_map/ppermute | solution.py:20
  216.5 18.5 %collective-permute-start.26 = (bf16[384,1152]{1,0:T(8,128)(2,1)S(1)}, bf16[384,1152]{1,0:T(8,128)(2,1)S(1)}, u32[]{:S(2)}, u32[]{:S(2)}) collective-permute-start(bf16[384,1152]{1,0:T(8,128)(2,1)S(1)} %pad_maximum_fusion.4), channel_id=1, source_target_pairs={{0,32},{32,64},{64,96},{96,0},{1,33},{33,65},{65,97},{97,1},{2,34}... | collective-permute-start | bytes 2654216 | tf_op jit(solution)/shard_map/ppermute | solution.py:20
  218.1 19.3 %collective-permute-start.28 = (bf16[384,1152]{1,0:T(8,128)(2,1)S(1)}, bf16[384,1152]{1,0:T(8,128)(2,1)S(1)}, u32[]{:S(2)}, u32[]{:S(2)}) collective-permute-start(bf16[384,1152]{1,0:T(8,128)(2,1)S(1)} %pad_maximum_fusion.5), channel_id=1, source_target_pairs={{0,96},{32,0},{64,32},{96,64},{1,97},{33,1},{65,33},{97,65},{2,98}... | collective-permute-start | bytes 2654216 | tf_op jit(solution)/shard_map/ppermute | solution.py:20
  239.2 19.0 %collective-permute-start.29 = (bf16[192,1152]{1,0:T(8,128)(2,1)S(1)}, bf16[192,1152]{1,0:T(8,128)(2,1)S(1)}, u32[]{:S(2)}, u32[]{:S(2)}) collective-permute-start(bf16[192,1152]{1,0:T(8,128)(2,1)S(1)} %get-tuple-element.52), channel_id=1, source_target_pairs={{16,2},{2,16},{17,3},{3,17},{20,6},{6,20},{21,7},{7,21},{24,10},{1... | collective-permute-start | bytes 1327112 | tf_op jit(solution)/shard_map/ppermute | solution.py:229
  241.2 17.0 %collective-permute-start.30 = (bf16[192,1152]{1,0:T(8,128)(2,1)S(1)}, bf16[192,1152]{1,0:T(8,128)(2,1)S(1)}, u32[]{:S(2)}, u32[]{:S(2)}) collective-permute-start(bf16[192,1152]{1,0:T(8,128)(2,1)S(1)} %get-tuple-element.53), channel_id=1, source_target_pairs={{16,0},{2,18},{0,2},{18,16},{17,1},{3,19},{1,3},{19,17},{20,4},{6,... | collective-permute-start | bytes 1327112 | tf_op jit(solution)/shard_map/ppermute | solution.py:228
